TPU v7x, 256 devices: a whole 4x4x8 slice. The times are simulated.
256 devices in a mesh: lat: 32 (over z_lo, y, core), lon: 8 (over x, z_hi).
Axes of the slice: x: 4, y: 4, z: 8 (z_hi: 2, z_lo: 4; z = z_hi * 4 + z_lo), core: 2. Of those that a mesh axis runs over, the one named last changes fastest.
Arguments:
- field: float32 [128, 1440, 256], P('lat', 'lon'), may hold values from -6 to 6
- legendre: float32 [512, 720, 128], P('lat'), may hold values from -1 to 1, as said below
- shifts: int32 [128, 20], P('lat'), may hold values from -16 to 16
- psi: float32 [128, 20, 9], P('lat'), may hold values from -1.3 to 1.3
- kernel_weight: float32 [9, 32, 256], replicated, may hold values from -0.375 to 0.375
Outputs:
- coefficients: float32 [512, 720, 2, 256], P('lat', None, None, 'lon')
- convolved: float32 [128, 1440, 256], P('lat', 'lon')
Inputs may be any that keep to these rules, and one draw needn't show every extreme that they name: `legendre`: zero where the degree is below the order.
All inputs are finite; a program needn't handle non-finite values.
Results may differ from a plain program's by a relative error of at most 0.0001.
Values sent between devices are 32-bit elements; how exact they have to be, the bound alone decides.
A program may use at most 128 MiB of HBM per device.

v0:
```python
import jax
import jax.numpy as jnp
import ml_dtypes
import numpy as np
from jax import lax
from jax.experimental import pallas as pl
from jax.experimental.pallas import tpu as pltpu
from jax.sharding import PartitionSpec as P

LON = 1440
ORDERS = 512
SLAB = 180
PAD = 184
GW = 32
KERNELS = 9
SLOTS = 20
RADIUS = 2
REACH = 16
STRIPS = 12
SPAN = 232
MESH = pl.DeviceIdType.MESH
F32 = jnp.float32
BF16 = jnp.bfloat16
ORDER_OF = [0, 4, 8, 12, 2, 6, 10, 14, 1, 3, 5, 7, 9, 11, 13, 15]


def two_parts(table):
    table = np.asarray(table, np.float32)
    high = table.astype(ml_dtypes.bfloat16)
    low = (table - high.astype(np.float32)).astype(ml_dtypes.bfloat16)
    return np.stack([high, low])


def fourier_tables():
    even, odd = [], []
    for half in range(2):
        j = SLAB * half + np.arange(PAD)
        live = (np.arange(PAD) < SLAB).astype(np.float64)

        def rows(orders, lead):
            turn = (np.asarray(orders)[:, None] * (j[None, :] + lead)) % LON
            angle = turn * (2.0 * np.pi / LON)
            both = np.stack([np.cos(angle), -np.sin(angle)], axis=1) * live
            return both.reshape(-1, PAD)

        owner = np.arange(32)[:, None] * 16
        zero = (owner + np.arange(0, 16, 4)).reshape(-1)
        two = (owner + np.arange(2, 16, 4)).reshape(-1)
        ones = (owner + np.arange(1, 16, 2)).reshape(-1)
        even.append(two_parts(np.concatenate([rows(zero, 0), rows(two, 0)])))
        odd.append(two_parts(np.concatenate([rows(ones, 0), rows(ones, 360)], axis=1)))
    return np.stack(even), np.stack(odd)


def split(value):
    high = value.astype(BF16)
    return high, (value - high.astype(F32)).astype(BF16)


def main_kernel(
    shifts, psi, field, weight, even, odd,
    conv, lhs,
    g, e, f, pk, xr, sp, r, gh, gl, bdh, bdl, te, to, es,
    load_sem, table_sem, s1_send, s1_recv, h_send, h_recv, c_send, c_recv, s3_send, s3_recv, own_sem,
):
    lat = lax.axis_index("lat")
    lon = lax.axis_index("lon")
    x, half = lon // 2, lon % 2
    z_lo, y, core = lat // 8, (lat // 2) % 4, lat % 2
    right = lax.rem(lon + 1, 8)
    left = lax.rem(lon + 7, 8)

    load = pltpu.make_async_copy(field, g.at[pl.ds(2, 4)], load_sem)
    load.start()
    load_even = pltpu.make_async_copy(even.at[half], te, table_sem.at[0])
    load_odd = pltpu.make_async_copy(odd.at[half], to, table_sem.at[1])
    load_even.start()
    load_odd.start()

    barrier = pltpu.get_barrier_semaphore()

    def greet(step, carry):
        peer = lax.rem(lat + lax.rem(step, 32), 32)
        column = 2 * x + lax.rem(half + step // 32, 2)
        pl.semaphore_signal(barrier, inc=1, device_id=(peer, column), device_id_type=MESH)
        return carry

    lax.fori_loop(1, 64, greet, 0)
    for step in range(1, 4):
        pl.semaphore_signal(
            barrier, inc=1, device_id=(lat, 2 * lax.rem(x + step, 4) + half), device_id_type=MESH
        )
    outer = jnp.where(half == 1, right, left)
    pl.semaphore_signal(barrier, inc=1, device_id=(lat, outer), device_id_type=MESH)

    load.wait()
    es[0] = g[2:6, 0:REACH, :]
    es[1] = g[2:6, SLAB - REACH : SLAB, :]
    lane_block = lax.broadcasted_iota(jnp.int32, (8, 128), 1) // 32

    def pack(strip, carry):
        at = pl.ds(pl.multiple_of(strip * 8, 8), 8)
        for tile in range(2):
            rows = [g[2 + a, at, tile * 128 : tile * 128 + 128] for a in range(4)]
            for q in range(4):
                made = rows[q] if q else rows[0]
                for a in range(4):
                    if a != q:
                        moved = pltpu.roll(rows[a], ((a - q) * 32) % 128, 1)
                        made = jnp.where(lane_block == a, moved, made)
                pk[tile * 4 + q, at, :] = made
        return carry

    lax.fori_loop(0, PAD // 8, pack, 0)

    pl.semaphore_wait(barrier, 63 + 3 + 1)

    sends = []
    for turn in range(2):
        chunk = lax.rem(half + 1 + turn, 2)
        for step in (2, 1, 3):
            there = lax.rem(x + step, 4)
            copy = pltpu.make_async_remote_copy(
                src_ref=pk.at[2 * there + chunk],
                dst_ref=xr.at[turn, x],
                send_sem=s1_send.at[turn, step - 1],
                recv_sem=s1_recv.at[turn, step - 1],
                device_id=(lat, 2 * there + half),
                device_id_type=MESH,
            )
            copy.start()
            sends.append(copy)
        if turn == 0:
            edges = []
            for side, there in ((1, left), (0, right)):
                copy = pltpu.make_async_remote_copy(
                    src_ref=es.at[1 - side],
                    dst_ref=e.at[side, pl.ds(2, 4)],
                    send_sem=h_send.at[side],
                    recv_sem=h_recv.at[side],
                    device_id=(lat, there),
                    device_id_type=MESH,
                )
                copy.start()
                edges.append(copy)
    for turn in range(2):
        chunk = lax.rem(half + 1 + turn, 2)
        xr[turn, x] = pk[2 * x + chunk]

    up, down = lax.rem(lat + 1, 32), lax.rem(lat + 31, 32)

    def row_copies(buffer, index, send, recv):
        return (
            pltpu.make_async_remote_copy(
                src_ref=buffer.at[index + (pl.ds(4, 2),)],
                dst_ref=buffer.at[index + (pl.ds(0, 2),)],
                send_sem=send.at[0], recv_sem=recv.at[0],
                device_id=(up, lon), device_id_type=MESH,
            ),
            pltpu.make_async_remote_copy(
                src_ref=buffer.at[index + (pl.ds(2, 2),)],
                dst_ref=buffer.at[index + (pl.ds(6, 2),)],
                send_sem=send.at[1], recv_sem=recv.at[1],
                device_id=(down, lon), device_id_type=MESH,
            ),
        )

    halo = [
        row_copies(g, (), c_send.at[0], c_recv.at[0]),
        row_copies(e, (0,), c_send.at[1], c_recv.at[1]),
        row_copies(e, (1,), c_send.at[2], c_recv.at[2]),
    ]

    def start_rows(pair):
        @pl.when(lat < 31)
        def _():
            pair[0].start()

        @pl.when(lat > 0)
        def _():
            pair[1].start()

    start_rows(halo[0])

    @pl.when(lat == 0)
    def _():
        g[0:2] = jnp.zeros((2, PAD, 256), F32)
        e[:, 0:2] = jnp.zeros((2, 2, REACH, 256), F32)

    @pl.when(lat == 31)
    def _():
        g[6:8] = jnp.zeros((2, PAD, 256), F32)
        e[:, 6:8] = jnp.zeros((2, 2, REACH, 256), F32)

    group = lax.broadcasted_iota(jnp.int32, (GW, 256), 1) // GW

    def spread(k, carry):
        high, low = split(weight[k])
        high, low = high.astype(F32), low.astype(F32)
        for at in range(8):
            rows = pl.ds(pl.multiple_of(k * 256 + at * GW, GW), GW)
            bdh[rows, :] = jnp.where(group == at, high, 0.0).astype(BF16)
            bdl[rows, :] = jnp.where(group == at, low, 0.0).astype(BF16)
        return carry

    lax.fori_loop(0, KERNELS, spread, 0)
    load_even.wait()
    load_odd.wait()

    def transform(turn):
        s0, s1, s2, s3 = (xr[turn, i] for i in range(4))
        p02, p13 = s0 + s2, s1 + s3
        for at, value in ((0, p02 + p13), (1, p02 - p13)):
            high, low = split(value)
            both = jnp.concatenate([high, low], axis=1)
            rows = pl.ds(at * 256, 256)
            first = jnp.dot(te[0, rows, :], both, preferred_element_type=F32)
            second = jnp.dot(te[1, rows, :], high, preferred_element_type=F32)
            total = first[:, :128] + first[:, 128:] + second
            sp[turn, :, at * 8 : at * 8 + 8, :] = total.reshape(32, 8, 128)
        high, low = split(jnp.concatenate([s0 - s2, s1 - s3], axis=0))
        both = jnp.concatenate([high, low], axis=1)
        first = jnp.dot(to[0], both, preferred_element_type=F32)
        second = jnp.dot(to[1], high, preferred_element_type=F32)
        total = first[:, :128] + first[:, 128:] + second
        sp[turn, :, 16:32, :] = total.reshape(32, 16, 128)

    mine = half * 32 + lat

    def scatter(turn):
        column = 2 * x + lax.rem(half + 1 + turn, 2)

        def send(step, carry):
            there = (
                lax.rem(z_lo + step // 8, 4) * 8
                + lax.rem(y + lax.rem(step, 8) // 2, 4) * 2
                + lax.rem(core + step, 2)
            )
            pltpu.make_async_remote_copy(
                src_ref=sp.at[turn, there],
                dst_ref=r.at[mine],
                send_sem=s3_send,
                recv_sem=s3_recv,
                device_id=(there, column),
                device_id_type=MESH,
            ).start()
            return carry

        lax.fori_loop(turn, 32, send, 0)

    for turn in range(2):
        for copy in sends[turn * 3 : turn * 3 + 3]:
            copy.wait_recv()
        transform(turn)
        if turn == 0:
            for copy in edges:
                copy.wait_recv()
            start_rows(halo[1])
            start_rows(halo[2])
        scatter(turn)
    own = pltpu.make_async_copy(sp.at[1, lat], r.at[mine], own_sem)
    own.start()

    @pl.when(lat > 0)
    def _():
        for pair in halo:
            pair[0].wait_recv()

    @pl.when(lat < 31)
    def _():
        for pair in halo:
            pair[1].wait_recv()

    for row in range(8):
        for h in range(2):
            lanes = slice(h * 128, h * 128 + 128)
            f[h, row, 0:REACH, :] = e[0, row, :, lanes]
            f[h, row, REACH : REACH + SLAB, :] = g[row, 0:SLAB, lanes]
            f[h, row, REACH + SLAB : 2 * REACH + SLAB, :] = e[1, row, :, lanes]
            f[h, row, 2 * REACH + SLAB : SPAN, :] = jnp.zeros((SPAN - 2 * REACH - SLAB, 128), F32)

    def row_conv(a, carry):
        def strip(at, inner):
            sums = [jnp.zeros((16, 256), F32) for _ in range(KERNELS)]
            for s in range(SLOTS):
                begin = at * 16 + REACH + shifts[a, s]
                taken = jnp.concatenate([f[h, a + s % 5, pl.ds(begin, 16), :] for h in range(2)], axis=1)
                for k in range(KERNELS):
                    sums[k] = sums[k] + psi[a, s * KERNELS + k] * taken
            rows = pl.ds(pl.multiple_of(at * 16, 16), 16)
            for k in range(KERNELS):
                high, low = split(sums[k])
                gh[rows, k * 256 : k * 256 + 256] = high
                gl[rows, k * 256 : k * 256 + 256] = low
            return inner

        lax.fori_loop(0, STRIPS, strip, 0)
        total = jnp.dot(gh[...], bdh[...], preferred_element_type=F32)
        total += jnp.dot(gl[...], bdh[...], preferred_element_type=F32)
        total += jnp.dot(gh[...], bdl[...], preferred_element_type=F32)
        conv[a] = total[:SLAB]
        return carry

    lax.fori_loop(0, 4, row_conv, 0)

    own.wait()
    everyone = r.at[pl.ds(0, 63)]
    pltpu.make_async_copy(everyone, everyone, s3_recv).wait()
    from_row = lax.broadcasted_iota(jnp.int32, (128, 128), 0)
    to_lane = lax.broadcasted_iota(jnp.int32, (128, 128), 1)
    lane_of = (from_row % 32) * 4 + from_row // 32
    reorder = jnp.where(to_lane == lane_of, 1.0, 0.0).astype(BF16)
    block = lax.broadcasted_iota(jnp.int32, (32, 128), 1) // 32
    for quad in range(8):
        parts = [r[0:32, quad * 4 + i, :] + r[32:64, quad * 4 + i, :] for i in range(4)]
        turned = jnp.concatenate(parts, axis=0).T
        rows = [turned[a * 32 : a * 32 + 32, :] for a in range(4)]
        made = []
        for i in range(4):
            one = rows[i]
            for a in range(4):
                if a != i:
                    one = jnp.where(block == a, pltpu.roll(rows[a], ((a - i) * 32) % 128, 1), one)
            made.append(one)
        high, low = split(jnp.concatenate(made, axis=0))
        high = jnp.dot(high, reorder, preferred_element_type=F32).astype(BF16)
        low = jnp.dot(low, reorder, preferred_element_type=F32).astype(BF16)
        for n in range(2):
            order = ORDER_OF[quad * 2 + n]
            lhs[order, 0:64, :] = high[n * 64 : n * 64 + 64]
            lhs[order, 64:128, :] = low[n * 64 : n * 64 + 64]

    for copy in sends:
        copy.wait_send()
    for copy in edges:
        copy.wait_send()

    @pl.when(lat < 31)
    def _():
        for pair in halo:
            pair[0].wait_send()

    @pl.when(lat > 0)
    def _():
        for pair in halo:
            pair[1].wait_send()

    pltpu.make_async_copy(everyone, everyone, s3_send).wait()


def legendre_kernel(lhs, legendre, out):
    high, low = split(legendre[0])
    right = jnp.concatenate([high, low], axis=1)
    top, bottom = lhs[0, 0:64, :], lhs[0, 64:128, :]
    left = jnp.concatenate(
        [
            jnp.concatenate([top, top], axis=1),
            jnp.concatenate([bottom, jnp.zeros_like(bottom)], axis=1),
        ],
        axis=0,
    )
    both = lax.dot_general(left, right, (((1,), (1,)), ((), ())), preferred_element_type=F32)
    out[0] = both[0:64] + both[64:128]


def shards(field, legendre, shifts, psi, kernel_weight):
    even, odd = fourier_tables()
    padded = jnp.pad(field, ((0, 0), (0, PAD - SLAB), (0, 0)))
    vmem = pl.BlockSpec(memory_space=pltpu.VMEM)
    smem = pl.BlockSpec(memory_space=pltpu.SMEM)
    hbm = pl.BlockSpec(memory_space=pl.ANY)
    dma = pltpu.SemaphoreType.DMA
    conv, lhs = pl.pallas_call(
        main_kernel,
        out_shape=(
            jax.ShapeDtypeStruct((4, SLAB, 256), F32),
            jax.ShapeDtypeStruct((16, 128, 128), BF16),
        ),
        in_specs=[smem, smem, hbm, vmem, hbm, hbm],
        out_specs=(vmem, vmem),
        scratch_shapes=[
            pltpu.VMEM((8, PAD, 256), F32),
            pltpu.VMEM((2, 8, REACH, 256), F32),
            pltpu.VMEM((2, 8, SPAN, 128), F32),
            pltpu.VMEM((8, PAD, 128), F32),
            pltpu.VMEM((2, 4, PAD, 128), F32),
            pltpu.VMEM((2, 32, 32, 128), F32),
            pltpu.VMEM((64, 32, 128), F32),
            pltpu.VMEM((16 * STRIPS, KERNELS * 256), BF16),
            pltpu.VMEM((16 * STRIPS, KERNELS * 256), BF16),
            pltpu.VMEM((KERNELS * 256, 256), BF16),
            pltpu.VMEM((KERNELS * 256, 256), BF16),
            pltpu.VMEM((2, 512, PAD), BF16),
            pltpu.VMEM((2, 512, 2 * PAD), BF16),
            pltpu.VMEM((2, 4, REACH, 256), F32),
            dma,
            dma((2,)),
            dma((2, 3)),
            dma((2, 3)),
            dma((2,)),
            dma((2,)),
            dma((3, 2)),
            dma((3, 2)),
            dma,
            dma,
            dma,
        ],
        compiler_params=pltpu.CompilerParams(
            collective_id=0, has_side_effects=True, vmem_limit_bytes=40 * 1024 * 1024
        ),
        cost_estimate=pl.CostEstimate(flops=4_000_000_000, bytes_accessed=8_000_000, transcendentals=0),
        name="spectrum_and_convolution",
    )(shifts, psi.reshape(4, SLOTS * KERNELS), padded, kernel_weight, jnp.asarray(even), jnp.asarray(odd))
    coefficients = pl.pallas_call(
        legendre_kernel,
        grid=(16,),
        out_shape=jax.ShapeDtypeStruct((16, 64, 720), F32),
        in_specs=[
            pl.BlockSpec((1, 128, 128), lambda m: (m, 0, 0)),
            pl.BlockSpec((1, 720, 128), lambda m: (m, 0, 0)),
        ],
        out_specs=pl.BlockSpec((1, 64, 720), lambda m: (m, 0, 0)),
        compiler_params=pltpu.CompilerParams(vmem_limit_bytes=16 * 1024 * 1024),
        cost_estimate=pl.CostEstimate(flops=800_000_000, bytes_accessed=10_000_000, transcendentals=0),
        name="legendre",
    )(lhs, legendre)
    coefficients = coefficients.reshape(16, 2, GW, 720).transpose(0, 3, 1, 2)
    return coefficients, conv


def solution(mesh):
    placed = (
        P("lat", "lon", None),
        P("lat", None, None),
        P("lat", None),
        P("lat", None, None),
        P(),
    )
    return jax.shard_map(
        shards,
        mesh=mesh,
        in_specs=placed,
        out_specs=(P("lat", None, None, "lon"), P("lat", "lon", None)),
        check_vma=False,
    )
```

profile of v0, /device:TPU:59, one launch (start us, length us, event | category | flops | bytes accessed | tf_op | source)
XLA Modules:
  0.0 69.5 jit_solution(17803018126966135808)
XLA Ops:
  0.6 0.8 %copy.12 = f32[4,20,9]{2,1,0:T(8,128)S(1)} copy(f32[4,20,9]{1,0,2:T(4,128)} %param.10) | data formatting | bytes 5760 | tf_op args[3]
  1.5 0.1 reshape.10.psi
  1.6 1.3 %copy.13 = f32[4,180,256]{2,1,0:T(8,128)S(1)} copy(f32[4,180,256]{2,0,1:T(4,128)} %param.7) | data formatting | bytes 1474560 | tf_op args[0]
  2.8 0.0 slice-start
  2.8 0.1 pad.4.field
  2.9 0.0 copy-start
  2.9 1.1 %copy-done = f32[9,32,256]{2,1,0:T(8,128)S(1)} copy-done((f32[9,32,256]{2,1,0:T(8,128)S(1)}, f32[9,32,256]{2,1,0:T(8,128)}, u32[]{:S(2)}) %copy-start) | copy-done | bytes 294936
  4.0 0.0 copy-start.1
  4.0 0.8 %copy-done.1 = s32[4,20]{1,0:T(4,128)S(1)} copy-done((s32[4,20]{1,0:T(4,128)S(1)}, s32[4,20]{1,0:T(4,128)}, u32[]{:S(2)}) %copy-start.1) | copy-done | bytes 344
  4.9 0.0 copy-start.2
  4.9 1.4 %copy-done.2 = bf16[2,2,512,368]{3,2,1,0:T(8,128)(2,1)S(1)} copy-done((bf16[2,2,512,368]{3,2,1,0:T(8,128)(2,1)S(1)}, bf16[2,2,512,368]{3,2,1,0:T(8,128)(2,1)}, u32[]{:S(2)}) %copy-start.2) | copy-done | bytes 1507352
  6.3 0.0 copy-start.3
  6.3 1.2 %copy-done.3 = bf16[2,2,512,184]{3,2,1,0:T(8,128)(2,1)S(1)} copy-done((bf16[2,2,512,184]{3,2,1,0:T(8,128)(2,1)S(1)}, bf16[2,2,512,184]{3,2,1,0:T(8,128)(2,1)}, u32[]{:S(2)}) %copy-start.3) | copy-done | bytes 753688
  7.5 0.0 slice-start.1
  7.5 53.0 %spectrum_and_convolution.1 = (f32[4,180,256]{2,1,0:T(8,128)S(1)}, bf16[16,128,128]{2,1,0:T(8,128)(2,1)S(1)}) custom-call(s32[4,20]{1,0:T(4,128)S(1)} %copy-done.1, f32[4,180]{1,0:T(4,128)S(1)} %reshape.10.psi, f32[4,184,256]{2,1,0:T(8,128)S(1)} %pad.4.field, f32[9,32,256]{2,1,0:T(8,128)S(1)} %copy-done, bf16[2,2,512,184]{3,2,1,0:T(8,128)(2,1)S(1)} %copy-done.3, ...), custom_call_target="tpu_custom_call" | custom-call | flops 4000000000 | bytes 8000000 | tf_op jit(solution)/shard_map/spectrum_and_convolution/pallas_call | solution.py:373
  60.5 1.1 %copy.14 = f32[4,180,256]{2,0,1:T(4,128)} copy(f32[4,180,256]{2,1,0:T(8,128)S(1)} %get-tuple-element.9) | data formatting | bytes 1474560
  61.6 0.0 slice-done
  61.6 0.0 slice-done.1
  61.6 7.9 %legendre.2 = f32[16,64,720]{2,1,0:T(8,128)} custom-call(bf16[16,128,128]{2,1,0:T(8,128)(2,1)S(1)} %get-tuple-element.4.lhs, f32[16,720,128]{2,1,0:T(8,128)S(1)} %bitcast.4), custom_call_target="tpu_custom_call" | custom-call | flops 800000000 | bytes 10000000 | tf_op jit(solution)/shard_map/legendre/pallas_call | solution.py:414
  (1 shorter events, 0.0 us)
Async XLA Ops:
  2.8 58.8 %slice-start = ((s8[5898240]{0:T(1024)(128)(4,1)}), s8[4194304]{0:T(1024)(128)(4,1)S(1)}, s32[]{:S(2)}) async-start(s8[5898240]{0:T(1024)(128)(4,1)} %bitcast.3), calls=%async_computation | async-start | bytes 8388608
  2.9 1.1 %copy-start = (f32[9,32,256]{2,1,0:T(8,128)S(1)}, f32[9,32,256]{2,1,0:T(8,128)}, u32[]{:S(2)}) copy-start(f32[9,32,256]{2,1,0:T(8,128)} %weight.1) | copy-start | bytes 884740
  4.0 0.8 %copy-start.1 = (s32[4,20]{1,0:T(4,128)S(1)}, s32[4,20]{1,0:T(4,128)}, u32[]{:S(2)}) copy-start(s32[4,20]{1,0:T(4,128)} %shifts.1) | copy-start | bytes 964
  4.9 1.4 %copy-start.2 = (bf16[2,2,512,368]{3,2,1,0:T(8,128)(2,1)S(1)}, bf16[2,2,512,368]{3,2,1,0:T(8,128)(2,1)}, u32[]{:S(2)}) copy-start(bf16[2,2,512,368]{3,2,1,0:T(8,128)(2,1)} %constant.8.clone.odd) | copy-start | bytes 4521988
  6.3 1.2 %copy-start.3 = (bf16[2,2,512,184]{3,2,1,0:T(8,128)(2,1)S(1)}, bf16[2,2,512,184]{3,2,1,0:T(8,128)(2,1)}, u32[]{:S(2)}) copy-start(bf16[2,2,512,184]{3,2,1,0:T(8,128)(2,1)} %constant.7.clone.even) | copy-start | bytes 2260996
  7.5 54.1 %slice-start.1 = ((s8[5898240]{0:T(1024)(128)(4,1)}), s8[1703936]{0:T(1024)(128)(4,1)S(1)}, s32[]{:S(2)}) async-start(s8[5898240]{0:T(1024)(128)(4,1)} %bitcast.3), calls=%async_computation.1 | async-start | bytes 3407872
where the time goes:
time: 69.8 us; the launch traced here: 69.5 us
  Pallas kernels  60.9 us (87%)
  local copies, waits for them, and re-layouts  7.98 us (11%)
    pallas_call x1, Pallas kernels, shards(): pl.pallas_call(main_kernel, out_shape=(jax.ShapeDtypeStruct((4, SLAB, 256...  53 us
    pallas_call x1, Pallas kernels, shards(): pl.pallas_call(legendre_kernel, grid=(16,), out_shape=jax.ShapeDtypeStruc...  7.91 us
    unnamed x15, local copies, waits for them, and re-layouts  7.84 us

commit v1 on v0

--- a/solution.py
+++ b/solution.py
@@ -58,9 +58,9 @@
 
 
 def main_kernel(
-    shifts, psi, field, weight, even, odd,
-    conv, lhs,
-    g, e, f, pk, xr, sp, r, gh, gl, bdh, bdl, te, to, es,
+    shifts_in, psi_in, field, weight_in, even, odd, legendre,
+    conv, lhs, lp,
+    g, gh_rows, e, f, pk, xr, sp, r, gh, gl, bdh, bdl, te, to, es, weight, lf, turned_l, shifts, psi,
     load_sem, table_sem, s1_send, s1_recv, h_send, h_recv, c_send, c_recv, s3_send, s3_recv, own_sem,
 ):
     lat = lax.axis_index("lat")
@@ -70,12 +70,21 @@
     right = lax.rem(lon + 1, 8)
     left = lax.rem(lon + 7, 8)
 
-    load = pltpu.make_async_copy(field, g.at[pl.ds(2, 4)], load_sem)
-    load.start()
-    load_even = pltpu.make_async_copy(even.at[half], te, table_sem.at[0])
-    load_odd = pltpu.make_async_copy(odd.at[half], to, table_sem.at[1])
-    load_even.start()
-    load_odd.start()
+    loads = [
+        pltpu.make_async_copy(field.at[:, a, :], g.at[a], load_sem.at[a])
+        for a in range(4)
+    ]
+    tables = [
+        pltpu.make_async_copy(weight_in, weight, table_sem.at[0]),
+        pltpu.make_async_copy(even.at[half], te, table_sem.at[1]),
+        pltpu.make_async_copy(odd.at[half], to, table_sem.at[2]),
+        pltpu.make_async_copy(psi_in, psi, table_sem.at[3]),
+        pltpu.make_async_copy(shifts_in, shifts, table_sem.at[4]),
+        pltpu.make_async_copy(legendre, lf, table_sem.at[5]),
+    ]
+    for copy in loads + tables:
+        copy.start()
+    pk[:, SLAB:PAD, :] = jnp.zeros((8, PAD - SLAB, 128), F32)
 
     barrier = pltpu.get_barrier_semaphore()
 
@@ -93,25 +102,28 @@
     outer = jnp.where(half == 1, right, left)
     pl.semaphore_signal(barrier, inc=1, device_id=(lat, outer), device_id_type=MESH)
 
-    load.wait()
-    es[0] = g[2:6, 0:REACH, :]
-    es[1] = g[2:6, SLAB - REACH : SLAB, :]
-    lane_block = lax.broadcasted_iota(jnp.int32, (8, 128), 1) // 32
-
-    def pack(strip, carry):
-        at = pl.ds(pl.multiple_of(strip * 8, 8), 8)
+    for copy in loads:
+        copy.wait()
+    es[0] = g[:, 0:REACH, :]
+    es[1] = g[:, SLAB - REACH : SLAB, :]
+    def pack(at, count):
+        lane_block = lax.broadcasted_iota(jnp.int32, (count, 128), 1) // 32
         for tile in range(2):
-            rows = [g[2 + a, at, tile * 128 : tile * 128 + 128] for a in range(4)]
+            rows = [g[a, at, tile * 128 : tile * 128 + 128] for a in range(4)]
             for q in range(4):
-                made = rows[q] if q else rows[0]
+                made = rows[q]
                 for a in range(4):
                     if a != q:
                         moved = pltpu.roll(rows[a], ((a - q) * 32) % 128, 1)
                         made = jnp.where(lane_block == a, moved, made)
                 pk[tile * 4 + q, at, :] = made
+
+    def pack_strip(strip, carry):
+        pack(pl.ds(pl.multiple_of(strip * 8, 8), 8), 8)
         return carry
 
-    lax.fori_loop(0, PAD // 8, pack, 0)
+    lax.fori_loop(0, SLAB // 8, pack_strip, 0)
+    pack(pl.ds(SLAB - 4, 4), 4)
 
     pl.semaphore_wait(barrier, 63 + 3 + 1)
 
@@ -149,26 +161,26 @@
 
     up, down = lax.rem(lat + 1, 32), lax.rem(lat + 31, 32)
 
-    def row_copies(buffer, index, send, recv):
+    def row_copies(rows, above, below, send, recv):
         return (
             pltpu.make_async_remote_copy(
-                src_ref=buffer.at[index + (pl.ds(4, 2),)],
-                dst_ref=buffer.at[index + (pl.ds(0, 2),)],
+                src_ref=rows.at[pl.ds(2, 2)], dst_ref=above,
                 send_sem=send.at[0], recv_sem=recv.at[0],
                 device_id=(up, lon), device_id_type=MESH,
             ),
             pltpu.make_async_remote_copy(
-                src_ref=buffer.at[index + (pl.ds(2, 2),)],
-                dst_ref=buffer.at[index + (pl.ds(6, 2),)],
+                src_ref=rows.at[pl.ds(0, 2)], dst_ref=below,
                 send_sem=send.at[1], recv_sem=recv.at[1],
                 device_id=(down, lon), device_id_type=MESH,
             ),
         )
 
-    halo = [
-        row_copies(g, (), c_send.at[0], c_recv.at[0]),
-        row_copies(e, (0,), c_send.at[1], c_recv.at[1]),
-        row_copies(e, (1,), c_send.at[2], c_recv.at[2]),
+    halo = [row_copies(g, gh_rows.at[0], gh_rows.at[1], c_send.at[0], c_recv.at[0])] + [
+        row_copies(
+            e.at[side, pl.ds(2, 4)], e.at[side, pl.ds(0, 2)], e.at[side, pl.ds(6, 2)],
+            c_send.at[1 + side], c_recv.at[1 + side],
+        )
+        for side in range(2)
     ]
 
     def start_rows(pair):
@@ -184,14 +196,15 @@
 
     @pl.when(lat == 0)
     def _():
-        g[0:2] = jnp.zeros((2, PAD, 256), F32)
+        gh_rows[0] = jnp.zeros((2, SLAB, 256), F32)
         e[:, 0:2] = jnp.zeros((2, 2, REACH, 256), F32)
 
     @pl.when(lat == 31)
     def _():
-        g[6:8] = jnp.zeros((2, PAD, 256), F32)
+        gh_rows[1] = jnp.zeros((2, SLAB, 256), F32)
         e[:, 6:8] = jnp.zeros((2, 2, REACH, 256), F32)
 
+    tables[0].wait()
     group = lax.broadcasted_iota(jnp.int32, (GW, 256), 1) // GW
 
     def spread(k, carry):
@@ -204,8 +217,8 @@
         return carry
 
     lax.fori_loop(0, KERNELS, spread, 0)
-    load_even.wait()
-    load_odd.wait()
+    tables[1].wait()
+    tables[2].wait()
 
     def transform(turn):
         s0, s1, s2, s3 = (xr[turn, i] for i in range(4))
@@ -261,6 +274,21 @@
     own = pltpu.make_async_copy(sp.at[1, lat], r.at[mine], own_sem)
     own.start()
 
+    tables[5].wait()
+
+    def prepare(m, carry):
+        for block in range(6):
+            count = min(128, 720 - block * 128)
+            columns = slice(block * 128, block * 128 + count)
+            turned_l[block, :, 0:count] = lf[m, columns, :].T
+            for a in range(4):
+                high, low = split(turned_l[block, pl.ds(a, 32, stride=4), :])
+                lp[m, a * 32 : a * 32 + 32, columns] = high[:, :count]
+                lp[m, 128 + a * 32 : 160 + a * 32, columns] = low[:, :count]
+        return carry
+
+    lax.fori_loop(0, 16, prepare, 0)
+
     @pl.when(lat > 0)
     def _():
         for pair in halo:
@@ -272,12 +300,16 @@
             pair[1].wait_recv()
 
     for row in range(8):
+        source = g.at[row - 2] if 2 <= row < 6 else gh_rows.at[row // 6, row % 2]
         for h in range(2):
             lanes = slice(h * 128, h * 128 + 128)
             f[h, row, 0:REACH, :] = e[0, row, :, lanes]
-            f[h, row, REACH : REACH + SLAB, :] = g[row, 0:SLAB, lanes]
+            f[h, row, REACH : REACH + SLAB, :] = source[:, lanes]
             f[h, row, REACH + SLAB : 2 * REACH + SLAB, :] = e[1, row, :, lanes]
             f[h, row, 2 * REACH + SLAB : SPAN, :] = jnp.zeros((SPAN - 2 * REACH - SLAB, 128), F32)
+
+    tables[3].wait()
+    tables[4].wait()
 
     def row_conv(a, carry):
         def strip(at, inner):
@@ -286,7 +318,7 @@
                 begin = at * 16 + REACH + shifts[a, s]
                 taken = jnp.concatenate([f[h, a + s % 5, pl.ds(begin, 16), :] for h in range(2)], axis=1)
                 for k in range(KERNELS):
-                    sums[k] = sums[k] + psi[a, s * KERNELS + k] * taken
+                    sums[k] = sums[k] + psi[k, a, s] * taken
             rows = pl.ds(pl.multiple_of(at * 16, 16), 16)
             for k in range(KERNELS):
                 high, low = split(sums[k])
@@ -306,10 +338,6 @@
     own.wait()
     everyone = r.at[pl.ds(0, 63)]
     pltpu.make_async_copy(everyone, everyone, s3_recv).wait()
-    from_row = lax.broadcasted_iota(jnp.int32, (128, 128), 0)
-    to_lane = lax.broadcasted_iota(jnp.int32, (128, 128), 1)
-    lane_of = (from_row % 32) * 4 + from_row // 32
-    reorder = jnp.where(to_lane == lane_of, 1.0, 0.0).astype(BF16)
     block = lax.broadcasted_iota(jnp.int32, (32, 128), 1) // 32
     for quad in range(8):
         parts = [r[0:32, quad * 4 + i, :] + r[32:64, quad * 4 + i, :] for i in range(4)]
@@ -323,8 +351,6 @@
                     one = jnp.where(block == a, pltpu.roll(rows[a], ((a - i) * 32) % 128, 1), one)
             made.append(one)
         high, low = split(jnp.concatenate(made, axis=0))
-        high = jnp.dot(high, reorder, preferred_element_type=F32).astype(BF16)
-        low = jnp.dot(low, reorder, preferred_element_type=F32).astype(BF16)
         for n in range(2):
             order = ORDER_OF[quad * 2 + n]
             lhs[order, 0:64, :] = high[n * 64 : n * 64 + 64]
@@ -348,38 +374,51 @@
     pltpu.make_async_copy(everyone, everyone, s3_send).wait()
 
 
-def legendre_kernel(lhs, legendre, out):
-    high, low = split(legendre[0])
-    right = jnp.concatenate([high, low], axis=1)
-    top, bottom = lhs[0, 0:64, :], lhs[0, 64:128, :]
-    left = jnp.concatenate(
-        [
-            jnp.concatenate([top, top], axis=1),
-            jnp.concatenate([bottom, jnp.zeros_like(bottom)], axis=1),
-        ],
-        axis=0,
-    )
-    both = lax.dot_general(left, right, (((1,), (1,)), ((), ())), preferred_element_type=F32)
-    out[0] = both[0:64] + both[64:128]
+def legendre_kernel(lhs, lp, conv, out, moved, made, out_sem, move_sem):
+    moves = [pltpu.make_async_copy(conv.at[a], moved.at[:, a, :], move_sem.at[a]) for a in range(4)]
+    for copy in moves:
+        copy.start()
+
+    def leaving(m):
+        return pltpu.make_async_copy(made.at[m], out.at[m], out_sem.at[m])
+
+    def order(m, carry):
+        top, bottom = lhs[m, 0:64, :], lhs[m, 64:128, :]
+        left = jnp.concatenate(
+            [
+                jnp.concatenate([top, top], axis=1),
+                jnp.concatenate([bottom, jnp.zeros_like(bottom)], axis=1),
+            ],
+            axis=0,
+        )
+        both = jnp.dot(left, lp[m], preferred_element_type=F32)
+        made[m] = both[0:64] + both[64:128]
+        leaving(m).start()
+        return carry
+
+    lax.fori_loop(0, 16, order, 0, unroll=4)
+    for copy in moves:
+        copy.wait()
+    lax.fori_loop(0, 16, lambda m, carry: leaving(m).wait(), None)
 
 
 def shards(field, legendre, shifts, psi, kernel_weight):
     even, odd = fourier_tables()
-    padded = jnp.pad(field, ((0, 0), (0, PAD - SLAB), (0, 0)))
     vmem = pl.BlockSpec(memory_space=pltpu.VMEM)
-    smem = pl.BlockSpec(memory_space=pltpu.SMEM)
-    hbm = pl.BlockSpec(memory_space=pl.ANY)
+    hbm = pl.BlockSpec(memory_space=pltpu.HBM)
     dma = pltpu.SemaphoreType.DMA
-    conv, lhs = pl.pallas_call(
+    conv, lhs, prepared = pl.pallas_call(
         main_kernel,
         out_shape=(
-            jax.ShapeDtypeStruct((4, SLAB, 256), F32),
-            jax.ShapeDtypeStruct((16, 128, 128), BF16),
+            pltpu.VMEM((4, SLAB, 256), F32),
+            pltpu.VMEM((16, 128, 128), BF16),
+            pltpu.VMEM((16, 256, 720), BF16),
         ),
-        in_specs=[smem, smem, hbm, vmem, hbm, hbm],
-        out_specs=(vmem, vmem),
+        in_specs=[hbm] * 7,
+        out_specs=(vmem, vmem, vmem),
         scratch_shapes=[
-            pltpu.VMEM((8, PAD, 256), F32),
+            pltpu.VMEM((4, SLAB, 256), F32),
+            pltpu.VMEM((2, 2, SLAB, 256), F32),
             pltpu.VMEM((2, 8, REACH, 256), F32),
             pltpu.VMEM((2, 8, SPAN, 128), F32),
             pltpu.VMEM((8, PAD, 128), F32),
@@ -393,8 +432,13 @@
             pltpu.VMEM((2, 512, PAD), BF16),
             pltpu.VMEM((2, 512, 2 * PAD), BF16),
             pltpu.VMEM((2, 4, REACH, 256), F32),
-            dma,
-            dma((2,)),
+            pltpu.VMEM((KERNELS, GW, 256), F32),
+            pltpu.VMEM((16, 720, 128), F32),
+            pltpu.VMEM((6, 128, 128), F32),
+            pltpu.SMEM((4, SLOTS), jnp.int32),
+            pltpu.SMEM((KERNELS, 4, SLOTS), F32),
+            dma((4,)),
+            dma((6,)),
             dma((2, 3)),
             dma((2, 3)),
             dma((2,)),
@@ -406,26 +450,39 @@
             dma,
         ],
         compiler_params=pltpu.CompilerParams(
-            collective_id=0, has_side_effects=True, vmem_limit_bytes=40 * 1024 * 1024
+            collective_id=0, has_side_effects=True, vmem_limit_bytes=44 * 1024 * 1024
         ),
         cost_estimate=pl.CostEstimate(flops=4_000_000_000, bytes_accessed=8_000_000, transcendentals=0),
         name="spectrum_and_convolution",
-    )(shifts, psi.reshape(4, SLOTS * KERNELS), padded, kernel_weight, jnp.asarray(even), jnp.asarray(odd))
-    coefficients = pl.pallas_call(
+    )(
+        *(
+            pltpu.with_memory_space_constraint(value, pltpu.HBM)
+            for value in (
+                shifts,
+                psi.transpose(2, 0, 1),
+                field.transpose(1, 0, 2),
+                kernel_weight,
+                jnp.asarray(even),
+                jnp.asarray(odd),
+                legendre,
+            )
+        )
+    )
+    coefficients, moved = pl.pallas_call(
         legendre_kernel,
-        grid=(16,),
-        out_shape=jax.ShapeDtypeStruct((16, 64, 720), F32),
-        in_specs=[
-            pl.BlockSpec((1, 128, 128), lambda m: (m, 0, 0)),
-            pl.BlockSpec((1, 720, 128), lambda m: (m, 0, 0)),
-        ],
-        out_specs=pl.BlockSpec((1, 64, 720), lambda m: (m, 0, 0)),
-        compiler_params=pltpu.CompilerParams(vmem_limit_bytes=16 * 1024 * 1024),
+        out_shape=(
+            jax.ShapeDtypeStruct((16, 64, 720), F32),
+            jax.ShapeDtypeStruct((SLAB, 4, 256), F32),
+        ),
+        in_specs=[vmem, vmem, vmem],
+        out_specs=(hbm, hbm),
+        scratch_shapes=[pltpu.VMEM((16, 64, 720), F32), dma((16,)), dma((4,))],
+        compiler_params=pltpu.CompilerParams(vmem_limit_bytes=24 * 1024 * 1024),
         cost_estimate=pl.CostEstimate(flops=800_000_000, bytes_accessed=10_000_000, transcendentals=0),
         name="legendre",
-    )(lhs, legendre)
+    )(lhs, prepared, conv)
     coefficients = coefficients.reshape(16, 2, GW, 720).transpose(0, 3, 1, 2)
-    return coefficients, conv
+    return coefficients, moved.transpose(1, 0, 2)
 
 
 def solution(mesh):

time: 69.8 us -> 54.9 us (0.79)
  local copies, waits for them, and re-layouts: 7.98 us -> 0 us
  Pallas kernels: 60.9 us -> 54.2 us
    unnamed x15 -> x0, local copies, waits for them, and re-layouts: 7.84 us -> none
    pallas_call x2, Pallas kernels: 60.9 us -> 54.2 us  [the longest x1 51.7 us: shards(): pl.pallas_call(main_kernel, out_shape=(pltpu.VMEM((4, SLAB, 256), F32), p...]
where the time goes in v1:
time: 54.9 us; the launch traced here: 54.8 us
  Pallas kernels  54.2 us (99%)
  between operations  0.64 us (1%)
    pallas_call x1, Pallas kernels, shards(): pl.pallas_call(main_kernel, out_shape=(pltpu.VMEM((4, SLAB, 256), F32), p...  51.7 us
    pallas_call x1, Pallas kernels, shards(): pl.pallas_call(legendre_kernel, out_shape=(jax.ShapeDtypeStruct((16, 64,...  2.47 us

profile of v1, /device:TPU:59, one launch (start us, length us, event | category | flops | bytes accessed | tf_op | source)
XLA Modules:
  0.0 54.8 jit_solution(12175918459436385092)
XLA Ops:
  0.6 51.7 %spectrum_and_convolution.1 = (f32[4,180,256]{2,1,0:T(8,128)S(1)}, bf16[16,128,128]{2,1,0:T(8,128)(2,1)S(1)}, bf16[16,256,720]{2,1,0:T(8,128)(2,1)S(1)}) custom-call(s32[4,20]{1,0:T(4,128)} %shifts_in.1, f32[9,4,20]{2,1,0:T(4,128)} %bitcast.9, f32[180,4,256]{2,1,0:T(4,128)} %bitcast.7, f32[9,32,256]{2,1,0:T(8,128)} %weight_in.1, ...), custom_call_target="tpu_custom_call" | custom-call | flops 4000000000 | bytes 8000000 | tf_op jit(solution)/shard_map/spectrum_and_convolution/pallas_call | solution.py:410
  52.3 2.5 %legendre.3 = (f32[16,64,720]{2,1,0:T(8,128)}, f32[180,4,256]{2,1,0:T(4,128)}) custom-call(bf16[16,128,128]{2,1,0:T(8,128)(2,1)S(1)} %get-tuple-element.7.lhs, bf16[16,256,720]{2,1,0:T(8,128)(2,1)S(1)} %get-tuple-element.8.lp, f32[4,180,256]{2,1,0:T(8,128)S(1)} %get-tuple-element.9.conv), custom_call_target="tpu_custom_call" | custom-call | flops 800000000 | bytes 10000000 | tf_op jit(solution)/shard_map/legendre/pallas_call | solution.py:471

commit v2 on v1

--- a/solution.py
+++ b/solution.py
@@ -16,7 +16,8 @@
 SLOTS = 20
 RADIUS = 2
 REACH = 16
-STRIPS = 12
+STRIDE = 2 * RADIUS + 1
+ROWS = 192
 SPAN = 232
 MESH = pl.DeviceIdType.MESH
 F32 = jnp.float32
@@ -60,7 +61,7 @@
 def main_kernel(
     shifts_in, psi_in, field, weight_in, even, odd, legendre,
     conv, lhs, lp,
-    g, gh_rows, e, f, pk, xr, sp, r, gh, gl, bdh, bdl, te, to, es, weight, lf, turned_l, shifts, psi,
+    g, gh_rows, e, f, pk, xr, sp, r, taps_a, taps_b, mix_a, mix_b, te, to, es, weight, lf, turned_l, shifts, psi,
     load_sem, table_sem, s1_send, s1_recv, h_send, h_recv, c_send, c_recv, s3_send, s3_recv, own_sem,
 ):
     lat = lax.axis_index("lat")
@@ -204,19 +205,23 @@
         gh_rows[1] = jnp.zeros((2, SLAB, 256), F32)
         e[:, 6:8] = jnp.zeros((2, 2, REACH, 256), F32)
 
-    tables[0].wait()
-    group = lax.broadcasted_iota(jnp.int32, (GW, 256), 1) // GW
-
-    def spread(k, carry):
-        high, low = split(weight[k])
-        high, low = high.astype(F32), low.astype(F32)
-        for at in range(8):
-            rows = pl.ds(pl.multiple_of(k * 256 + at * GW, GW), GW)
-            bdh[rows, :] = jnp.where(group == at, high, 0.0).astype(BF16)
-            bdl[rows, :] = jnp.where(group == at, low, 0.0).astype(BF16)
+    mix_a[...] = jnp.zeros(mix_a.shape, BF16)
+    mix_b[...] = jnp.zeros(mix_b.shape, BF16)
+    tables[5].wait()
+
+    def prepare(m, carry):
+        for block in range(6):
+            count = min(128, 720 - block * 128)
+            columns = slice(block * 128, block * 128 + count)
+            turned_l[block, :, 0:count] = lf[m, columns, :].T
+            for a in range(4):
+                high, low = split(turned_l[block, pl.ds(a, 32, stride=4), :])
+                lp[m, a * 32 : a * 32 + 32, columns] = high[:, :count]
+                lp[m, 128 + a * 32 : 160 + a * 32, columns] = low[:, :count]
         return carry
 
-    lax.fori_loop(0, KERNELS, spread, 0)
+    lax.fori_loop(0, 16, prepare, 0, unroll=2)
+
     tables[1].wait()
     tables[2].wait()
 
@@ -245,9 +250,9 @@
 
         def send(step, carry):
             there = (
-                lax.rem(z_lo + step // 8, 4) * 8
-                + lax.rem(y + lax.rem(step, 8) // 2, 4) * 2
-                + lax.rem(core + step, 2)
+                lax.rem(z_lo + lax.rem(step, 4), 4) * 8
+                + lax.rem(y + lax.rem(step, 32) // 8, 4) * 2
+                + lax.rem(core + step // 4, 2)
             )
             pltpu.make_async_remote_copy(
                 src_ref=sp.at[turn, there],
@@ -274,21 +279,6 @@
     own = pltpu.make_async_copy(sp.at[1, lat], r.at[mine], own_sem)
     own.start()
 
-    tables[5].wait()
-
-    def prepare(m, carry):
-        for block in range(6):
-            count = min(128, 720 - block * 128)
-            columns = slice(block * 128, block * 128 + count)
-            turned_l[block, :, 0:count] = lf[m, columns, :].T
-            for a in range(4):
-                high, low = split(turned_l[block, pl.ds(a, 32, stride=4), :])
-                lp[m, a * 32 : a * 32 + 32, columns] = high[:, :count]
-                lp[m, 128 + a * 32 : 160 + a * 32, columns] = low[:, :count]
-        return carry
-
-    lax.fori_loop(0, 16, prepare, 0)
-
     @pl.when(lat > 0)
     def _():
         for pair in halo:
@@ -299,41 +289,62 @@
         for pair in halo:
             pair[1].wait_recv()
 
+    def place(row, h, at, value):
+        high = value.astype(BF16).astype(F32)
+        f[0, h, row, at : at + value.shape[0], :] = high
+        f[1, h, row, at : at + value.shape[0], :] = value - high
+
     for row in range(8):
         source = g.at[row - 2] if 2 <= row < 6 else gh_rows.at[row // 6, row % 2]
         for h in range(2):
             lanes = slice(h * 128, h * 128 + 128)
-            f[h, row, 0:REACH, :] = e[0, row, :, lanes]
-            f[h, row, REACH : REACH + SLAB, :] = source[:, lanes]
-            f[h, row, REACH + SLAB : 2 * REACH + SLAB, :] = e[1, row, :, lanes]
-            f[h, row, 2 * REACH + SLAB : SPAN, :] = jnp.zeros((SPAN - 2 * REACH - SLAB, 128), F32)
-
-    tables[3].wait()
-    tables[4].wait()
-
-    def row_conv(a, carry):
-        def strip(at, inner):
-            sums = [jnp.zeros((16, 256), F32) for _ in range(KERNELS)]
-            for s in range(SLOTS):
-                begin = at * 16 + REACH + shifts[a, s]
-                taken = jnp.concatenate([f[h, a + s % 5, pl.ds(begin, 16), :] for h in range(2)], axis=1)
-                for k in range(KERNELS):
-                    sums[k] = sums[k] + psi[k, a, s] * taken
-            rows = pl.ds(pl.multiple_of(at * 16, 16), 16)
-            for k in range(KERNELS):
-                high, low = split(sums[k])
-                gh[rows, k * 256 : k * 256 + 256] = high
-                gl[rows, k * 256 : k * 256 + 256] = low
-            return inner
-
-        lax.fori_loop(0, STRIPS, strip, 0)
-        total = jnp.dot(gh[...], bdh[...], preferred_element_type=F32)
-        total += jnp.dot(gl[...], bdh[...], preferred_element_type=F32)
-        total += jnp.dot(gh[...], bdl[...], preferred_element_type=F32)
-        conv[a] = total[:SLAB]
+            place(row, h, 0, e[0, row, :, lanes])
+            place(row, h, REACH, source[:, lanes])
+            place(row, h, REACH + SLAB, e[1, row, :, lanes])
+            f[:, h, row, 2 * REACH + SLAB : SPAN, :] = jnp.zeros((2, SPAN - 2 * REACH - SLAB, 128), F32)
+
+    for table in (tables[0], tables[3], tables[4]):
+        table.wait()
+    group = lax.broadcasted_iota(jnp.int32, (GW, 128), 1) // GW
+
+    def fill(a, quarter, taps, mix):
+        for d in range(STRIDE):
+            s = quarter * STRIDE + d
+            mixed = psi[0, a, s] * weight[0]
+            for k in range(1, KERNELS):
+                mixed = mixed + psi[k, a, s] * weight[k]
+            high = mixed.astype(BF16).astype(F32)
+            low = mixed - high
+            for at in range(8):
+                lanes = slice(at // 4 * 128, at // 4 * 128 + 128)
+                rows = slice(d * 256 + at * GW, d * 256 + at * GW + GW)
+                mix[0, rows, lanes] = jnp.where(group == at % 4, high[:, lanes], 0.0).astype(BF16)
+                mix[1, rows, lanes] = jnp.where(group == at % 4, low[:, lanes], 0.0).astype(BF16)
+            begin = REACH + shifts[a, s]
+            for p in range(2):
+                for h in range(2):
+                    lanes = slice(d * 256 + h * 128, d * 256 + h * 128 + 128)
+                    taps[p * ROWS : p * ROWS + ROWS, lanes] = f[p, h, a + d, pl.ds(begin, ROWS), :].astype(BF16)
+
+    def gather(a, taps, mix):
+        both = jnp.dot(taps[...], mix[0], preferred_element_type=F32)
+        total = both[:ROWS] + both[ROWS:]
+        total += jnp.dot(taps[0:ROWS, :], mix[1], preferred_element_type=F32)
+        conv[a] = conv[a] + total[:SLAB]
+
+    conv[...] = jnp.zeros(conv.shape, F32)
+    fill(0, 0, taps_a, mix_a)
+
+    def two_quarters(i, carry):
+        second = 2 * i + 1
+        fill(second // 4, lax.rem(second, 4), taps_b, mix_b)
+        gather(i // 2, taps_a, mix_a)
+        third = jnp.minimum(2 * i + 2, 15)
+        fill(third // 4, lax.rem(third, 4), taps_a, mix_a)
+        gather(second // 4, taps_b, mix_b)
         return carry
 
-    lax.fori_loop(0, 4, row_conv, 0)
+    lax.fori_loop(0, 8, two_quarters, 0)
 
     own.wait()
     everyone = r.at[pl.ds(0, 63)]
@@ -420,15 +431,15 @@
             pltpu.VMEM((4, SLAB, 256), F32),
             pltpu.VMEM((2, 2, SLAB, 256), F32),
             pltpu.VMEM((2, 8, REACH, 256), F32),
-            pltpu.VMEM((2, 8, SPAN, 128), F32),
+            pltpu.VMEM((2, 2, 8, SPAN, 128), F32),
             pltpu.VMEM((8, PAD, 128), F32),
             pltpu.VMEM((2, 4, PAD, 128), F32),
             pltpu.VMEM((2, 32, 32, 128), F32),
             pltpu.VMEM((64, 32, 128), F32),
-            pltpu.VMEM((16 * STRIPS, KERNELS * 256), BF16),
-            pltpu.VMEM((16 * STRIPS, KERNELS * 256), BF16),
-            pltpu.VMEM((KERNELS * 256, 256), BF16),
-            pltpu.VMEM((KERNELS * 256, 256), BF16),
+            pltpu.VMEM((2 * ROWS, STRIDE * 256), BF16),
+            pltpu.VMEM((2 * ROWS, STRIDE * 256), BF16),
+            pltpu.VMEM((2, STRIDE * 256, 256), BF16),
+            pltpu.VMEM((2, STRIDE * 256, 256), BF16),
             pltpu.VMEM((2, 512, PAD), BF16),
             pltpu.VMEM((2, 512, 2 * PAD), BF16),
             pltpu.VMEM((2, 4, REACH, 256), F32),

time: 54.9 us -> 50.7 us (0.923)
  the two profiles are of different devices: /device:TPU:59 before, /device:TPU:29 now
where the time goes in v2:
time: 50.7 us; the launch traced here: 50.6 us
  Pallas kernels  49.9 us (98%)
  between operations  0.64 us (1%)
    pallas_call x1, Pallas kernels, shards(): pl.pallas_call(main_kernel, out_shape=(pltpu.VMEM((4, SLAB, 256), F32), p...  47.5 us
    pallas_call x1, Pallas kernels, shards(): pl.pallas_call(legendre_kernel, out_shape=(jax.ShapeDtypeStruct((16, 64,...  2.47 us

profile of v2, /device:TPU:29, one launch (start us, length us, event | category | flops | bytes accessed | tf_op | source)
XLA Modules:
  0.0 50.6 jit_solution(7109745407664515192)
XLA Ops:
  0.6 47.5 %spectrum_and_convolution.1 = (f32[4,180,256]{2,1,0:T(8,128)S(1)}, bf16[16,128,128]{2,1,0:T(8,128)(2,1)S(1)}, bf16[16,256,720]{2,1,0:T(8,128)(2,1)S(1)}) custom-call(s32[4,20]{1,0:T(4,128)} %shifts_in.1, f32[9,4,20]{2,1,0:T(4,128)} %bitcast.9, f32[180,4,256]{2,1,0:T(4,128)} %bitcast.7, f32[9,32,256]{2,1,0:T(8,128)} %weight_in.1, ...), custom_call_target="tpu_custom_call" | custom-call | flops 4000000000 | bytes 8000000 | tf_op jit(solution)/shard_map/spectrum_and_convolution/pallas_call | solution.py:421
  48.1 2.5 %legendre.3 = (f32[16,64,720]{2,1,0:T(8,128)}, f32[180,4,256]{2,1,0:T(4,128)}) custom-call(bf16[16,128,128]{2,1,0:T(8,128)(2,1)S(1)} %get-tuple-element.7.lhs, bf16[16,256,720]{2,1,0:T(8,128)(2,1)S(1)} %get-tuple-element.8.lp, f32[4,180,256]{2,1,0:T(8,128)S(1)} %get-tuple-element.9.conv), custom_call_target="tpu_custom_call" | custom-call | flops 800000000 | bytes 10000000 | tf_op jit(solution)/shard_map/legendre/pallas_call | solution.py:482

commit v3 on v2

--- a/solution.py
+++ b/solution.py
@@ -107,11 +107,11 @@
         copy.wait()
     es[0] = g[:, 0:REACH, :]
     es[1] = g[:, SLAB - REACH : SLAB, :]
-    def pack(at, count):
+    def pack(at, count, parity):
         lane_block = lax.broadcasted_iota(jnp.int32, (count, 128), 1) // 32
         for tile in range(2):
             rows = [g[a, at, tile * 128 : tile * 128 + 128] for a in range(4)]
-            for q in range(4):
+            for q in (parity, parity + 2):
                 made = rows[q]
                 for a in range(4):
                     if a != q:
@@ -119,18 +119,27 @@
                         made = jnp.where(lane_block == a, moved, made)
                 pk[tile * 4 + q, at, :] = made
 
-    def pack_strip(strip, carry):
-        pack(pl.ds(pl.multiple_of(strip * 8, 8), 8), 8)
-        return carry
-
-    lax.fori_loop(0, SLAB // 8, pack_strip, 0)
-    pack(pl.ds(SLAB - 4, 4), 4)
+    def pack_half(parity):
+        def strip(at, carry):
+            pack(pl.ds(pl.multiple_of(at * 8, 8), 8), 8, parity)
+            return carry
+
+        lax.fori_loop(0, SLAB // 8, strip, 0, unroll=2)
+        pack(pl.ds(SLAB - 4, 4), 4, parity)
+
+    @pl.when(half == 0)
+    def _():
+        pack_half(1)
+
+    @pl.when(half == 1)
+    def _():
+        pack_half(0)
 
     pl.semaphore_wait(barrier, 63 + 3 + 1)
 
-    sends = []
-    for turn in range(2):
+    def exchange(turn):
         chunk = lax.rem(half + 1 + turn, 2)
+        copies = []
         for step in (2, 1, 3):
             there = lax.rem(x + step, 4)
             copy = pltpu.make_async_remote_copy(
@@ -142,24 +151,22 @@
                 device_id_type=MESH,
             )
             copy.start()
-            sends.append(copy)
-        if turn == 0:
-            edges = []
-            for side, there in ((1, left), (0, right)):
-                copy = pltpu.make_async_remote_copy(
-                    src_ref=es.at[1 - side],
-                    dst_ref=e.at[side, pl.ds(2, 4)],
-                    send_sem=h_send.at[side],
-                    recv_sem=h_recv.at[side],
-                    device_id=(lat, there),
-                    device_id_type=MESH,
-                )
-                copy.start()
-                edges.append(copy)
-    for turn in range(2):
-        chunk = lax.rem(half + 1 + turn, 2)
-        xr[turn, x] = pk[2 * x + chunk]
-
+            copies.append(copy)
+        return copies
+
+    sends = exchange(0)
+    edges = []
+    for side, there in ((1, left), (0, right)):
+        copy = pltpu.make_async_remote_copy(
+            src_ref=es.at[1 - side],
+            dst_ref=e.at[side, pl.ds(2, 4)],
+            send_sem=h_send.at[side],
+            recv_sem=h_recv.at[side],
+            device_id=(lat, there),
+            device_id_type=MESH,
+        )
+        copy.start()
+        edges.append(copy)
     up, down = lax.rem(lat + 1, 32), lax.rem(lat + 31, 32)
 
     def row_copies(rows, above, below, send, recv):
@@ -194,6 +201,19 @@
             pair[1].start()
 
     start_rows(halo[0])
+
+    @pl.when(half == 0)
+    def _():
+        pack_half(0)
+
+    @pl.when(half == 1)
+    def _():
+        pack_half(1)
+
+    sends += exchange(1)
+    for turn in range(2):
+        chunk = lax.rem(half + 1 + turn, 2)
+        xr[turn, x] = pk[2 * x + chunk]
 
     @pl.when(lat == 0)
     def _():
@@ -407,7 +427,7 @@
         leaving(m).start()
         return carry
 
-    lax.fori_loop(0, 16, order, 0, unroll=4)
+    lax.fori_loop(0, 16, order, 0, unroll=16)
     for copy in moves:
         copy.wait()
     lax.fori_loop(0, 16, lambda m, carry: leaving(m).wait(), None)

time: 50.7 us -> 50.3 us (level)
  no operation moved by 1% of the time
where the time goes in v3:
time: 50.3 us; the launch traced here: 50.2 us
  Pallas kernels  49.6 us (99%)
  between operations  0.64 us (1%)
    pallas_call x1, Pallas kernels, shards(): pl.pallas_call(main_kernel, out_shape=(pltpu.VMEM((4, SLAB, 256), F32), p...  47.5 us
    pallas_call x1, Pallas kernels, shards(): pl.pallas_call(legendre_kernel, out_shape=(jax.ShapeDtypeStruct((16, 64,...  2.1 us

profile of v3, /device:TPU:29, one launch (start us, length us, event | category | flops | bytes accessed | tf_op | source)
XLA Modules:
  0.0 50.2 jit_solution(1431701593485609652)
XLA Ops:
  0.6 47.5 %spectrum_and_convolution.1 = (f32[4,180,256]{2,1,0:T(8,128)S(1)}, bf16[16,128,128]{2,1,0:T(8,128)(2,1)S(1)}, bf16[16,256,720]{2,1,0:T(8,128)(2,1)S(1)}) custom-call(s32[4,20]{1,0:T(4,128)} %shifts_in.1, f32[9,4,20]{2,1,0:T(4,128)} %bitcast.9, f32[180,4,256]{2,1,0:T(4,128)} %bitcast.7, f32[9,32,256]{2,1,0:T(8,128)} %weight_in.1, ...), custom_call_target="tpu_custom_call" | custom-call | flops 4000000000 | bytes 8000000 | tf_op jit(solution)/shard_map/spectrum_and_convolution/pallas_call | solution.py:441
  48.1 2.1 %legendre.3 = (f32[16,64,720]{2,1,0:T(8,128)}, f32[180,4,256]{2,1,0:T(4,128)}) custom-call(bf16[16,128,128]{2,1,0:T(8,128)(2,1)S(1)} %get-tuple-element.7.lhs, bf16[16,256,720]{2,1,0:T(8,128)(2,1)S(1)} %get-tuple-element.8.lp, f32[4,180,256]{2,1,0:T(8,128)S(1)} %get-tuple-element.9.conv), custom_call_target="tpu_custom_call" | custom-call | flops 800000000 | bytes 10000000 | tf_op jit(solution)/shard_map/legendre/pallas_call | solution.py:502

commit v4 on v3

--- a/solution.py
+++ b/solution.py
@@ -83,7 +83,7 @@
         pltpu.make_async_copy(shifts_in, shifts, table_sem.at[4]),
         pltpu.make_async_copy(legendre, lf, table_sem.at[5]),
     ]
-    for copy in loads + tables:
+    for copy in loads:
         copy.start()
     pk[:, SLAB:PAD, :] = jnp.zeros((8, PAD - SLAB, 128), F32)
 
@@ -105,6 +105,8 @@
 
     for copy in loads:
         copy.wait()
+    for copy in tables:
+        copy.start()
     es[0] = g[:, 0:REACH, :]
     es[1] = g[:, SLAB - REACH : SLAB, :]
     def pack(at, count, parity):

time: 50.3 us -> 50.3 us (level)
  no operation moved by 1% of the time
where the time goes in v4:
time: 50.3 us; the launch traced here: 50.2 us
  Pallas kernels  49.6 us (99%)
  between operations  0.64 us (1%)
    pallas_call x1, Pallas kernels, shards(): pl.pallas_call(main_kernel, out_shape=(pltpu.VMEM((4, SLAB, 256), F32), p...  47.5 us
    pallas_call x1, Pallas kernels, shards(): pl.pallas_call(legendre_kernel, out_shape=(jax.ShapeDtypeStruct((16, 64,...  2.1 us

profile of v4, /device:TPU:29, one launch (start us, length us, event | category | flops | bytes accessed | tf_op | source)
XLA Modules:
  0.0 50.2 jit_solution(3559056494450954825)
XLA Ops:
  0.6 47.5 %spectrum_and_convolution.1 = (f32[4,180,256]{2,1,0:T(8,128)S(1)}, bf16[16,128,128]{2,1,0:T(8,128)(2,1)S(1)}, bf16[16,256,720]{2,1,0:T(8,128)(2,1)S(1)}) custom-call(s32[4,20]{1,0:T(4,128)} %shifts_in.1, f32[9,4,20]{2,1,0:T(4,128)} %bitcast.9, f32[180,4,256]{2,1,0:T(4,128)} %bitcast.7, f32[9,32,256]{2,1,0:T(8,128)} %weight_in.1, ...), custom_call_target="tpu_custom_call" | custom-call | flops 4000000000 | bytes 8000000 | tf_op jit(solution)/shard_map/spectrum_and_convolution/pallas_call | solution.py:443
  48.1 2.1 %legendre.3 = (f32[16,64,720]{2,1,0:T(8,128)}, f32[180,4,256]{2,1,0:T(4,128)}) custom-call(bf16[16,128,128]{2,1,0:T(8,128)(2,1)S(1)} %get-tuple-element.7.lhs, bf16[16,256,720]{2,1,0:T(8,128)(2,1)S(1)} %get-tuple-element.8.lp, f32[4,180,256]{2,1,0:T(8,128)S(1)} %get-tuple-element.9.conv), custom_call_target="tpu_custom_call" | custom-call | flops 800000000 | bytes 10000000 | tf_op jit(solution)/shard_map/legendre/pallas_call | solution.py:504
